TPU v7x, 32 devices: a whole 2x2x4 slice. The times are simulated.
32 devices in a mesh: groups: 2 (over y), fsdp: 4 (over z), dp: 2 (over x), pair: 2 (over core).
Axes of the slice: x: 2, y: 2, z: 4, core: 2. Of those that a mesh axis runs over, the one named last changes fastest.
Arguments:
- hidden_input: bfloat16 [4096, 8192], P(('groups', 'fsdp', 'dp', 'pair')), parts along dimension 0, may hold values from -6 to 6
- norm_gain_vector: float32 [8192], replicated, may hold values from 0.5 to 18, as said below
- value_matrix: bfloat16 [8192, 768], P('fsdp'), may hold values from -0.0625 to 0.0625
- adapter_down_map: bfloat16 [16384, 64], P(('groups', 'fsdp')), parts along dimension 0, may hold values from -0.0625 to 0.0625
- adapter_up_map: bfloat16 [128, 768], P('groups'), parts along dimension 0, may hold values from -5 to 5
- values_gradient: bfloat16 [4096, 768], P(('groups', 'fsdp', 'dp', 'pair')), parts along dimension 0, may hold values from -6 to 6
Outputs:
- grad_hidden: bfloat16 [4096, 8192], P(('groups', 'fsdp', 'dp', 'pair')), parts along dimension 0
- grad_down: float32 [16384, 64], P(('groups', 'fsdp')), parts along dimension 0
- grad_up: float32 [128, 768], P('groups'), parts along dimension 0
There are 2 independent parts, one for each index of `groups`. A program takes and returns all parts, laid end to end along the dimension named above; an argument that names none is the same for every part. Nothing has to cross between parts.
Inputs may be any that keep to these rules, and one draw needn't show every extreme that they name: `norm_gain_vector`: positive gains.
All inputs are finite; a program needn't handle non-finite values.
Results may differ from a plain program's by a relative error of at most 0.0085.
Values may be sent and summed in bfloat16 or wider, within the bound.
A program may use at most 64 MiB of HBM per device.

v0:
```python
import math
import jax
import jax.numpy as jnp
from jax import lax
from jax.sharding import PartitionSpec as P

MODEL_WIDTH = 8192
ADAPTER_RANK = 64
norm_eps = 1e-05
adapter_scale = 2.0


def contract_last(left, right):
    return lax.dot_general(
        left, right, (((1,), (1,)), ((), ())), preferred_element_type=jnp.float32
    )


def contract_leading(left, right):
    return lax.dot_general(
        left, right, (((0,), (0,)), ((), ())), preferred_element_type=jnp.float32
    )


def local(
    hidden_input, norm_gain_vector, value_matrix, adapter_down_map, adapter_up_map, values_gradient
):
    width = hidden_input.shape[1]
    stream = hidden_input.astype(jnp.float32)
    inv_rms = lax.rsqrt(jnp.mean(stream * stream, axis=1, keepdims=True) + norm_eps)
    normalized_input = (stream * inv_rms * norm_gain_vector).astype(jnp.bfloat16)
    upward_product = (
        adapter_scale
        * jnp.dot(values_gradient, adapter_up_map.T, preferred_element_type=jnp.float32)
    ).astype(jnp.bfloat16)
    every_values, every_upward = (
        lax.all_gather(values_gradient, "fsdp", axis=0, tiled=True),
        lax.all_gather(upward_product, "fsdp", axis=0, tiled=True),
    )
    columns = contract_last(every_values, value_matrix) + contract_last(
        every_upward, adapter_down_map
    )
    gradient_normalized = lax.all_to_all(
        columns.astype(jnp.bfloat16), "fsdp", split_axis=0, concat_axis=1, tiled=True
    )
    window = normalized_input
    latent_f = jnp.dot(
        window,
        lax.all_gather(adapter_down_map, "fsdp", axis=0, tiled=True),
        preferred_element_type=jnp.float32,
    )
    scaled = gradient_normalized.astype(jnp.float32) * norm_gain_vector
    grad_stream = inv_rms * scaled - stream * (inv_rms**3 / width) * jnp.sum(
        scaled * stream, axis=1, keepdims=True
    )
    latent_code = latent_f.astype(jnp.bfloat16)
    window = normalized_input
    down_shard = lax.psum_scatter(
        contract_leading(window, upward_product), "fsdp", scatter_dimension=0, tiled=True
    )
    up_portion = adapter_scale * contract_leading(latent_code, values_gradient)
    down_shard = lax.psum(down_shard, ("dp", "pair"))
    up_full = lax.psum(up_portion, ("fsdp", "dp", "pair"))
    total = lax.psum(jnp.sum(down_shard * down_shard), "fsdp") + jnp.sum(up_full * up_full)
    factor = jnp.minimum(1.0, 0.5 * math.sqrt(MODEL_WIDTH * ADAPTER_RANK) / jnp.sqrt(total))
    return (grad_stream.astype(jnp.bfloat16), factor * down_shard, factor * up_full)


def solution(mesh):
    return jax.shard_map(
        local,
        mesh=mesh,
        in_specs=(
            P(("groups", "fsdp", "dp", "pair"), None),
            P(),
            P("fsdp", None),
            P(("groups", "fsdp"), None),
            P("groups", None),
            P(("groups", "fsdp", "dp", "pair"), None),
        ),
        out_specs=(
            P(("groups", "fsdp", "dp", "pair"), None),
            P(("groups", "fsdp"), None),
            P("groups", None),
        ),
        check_vma=False,
    )
```

profile of v0, /device:TPU:0, one launch (start us, length us, event | category | flops | bytes accessed | tf_op | source)
XLA Modules:
  0.0 322.7 jit_solution(588120099054937987)
XLA Ops:
  7.2 21.6 %all_gather.9 = bf16[512,768]{1,0:T(8,128)(2,1)S(1)} all-gather(bf16[128,768]{1,0:T(8,128)(2,1)} %param.11), channel_id=1, replica_groups=mesh['groups'=2,'fsdp'=4,'dp'=2,'pair'=2] {'fsdp'}, dimensions={0}, use_global_device_ids=true | all-gather | bytes 983040 | tf_op jit(solution)/shard_map/all_gather | solution.py:37
  28.9 1.2 fusion.7
  30.1 12.0 %all_gather.10 = bf16[512,64]{0,1:T(8,128)(2,1)S(1)} all-gather(bf16[128,64]{0,1:T(8,128)(2,1)S(1)} %fusion.7), channel_id=1, replica_groups=mesh['groups'=2,'fsdp'=4,'dp'=2,'pair'=2] {'fsdp'}, dimensions={0}, use_global_device_ids=true | all-gather | bytes 81920 | tf_op jit(solution)/shard_map/all_gather | solution.py:38
  42.1 1.8 fusion.13
  43.9 0.7 add_convert_fusion
  44.6 46.4 %all_to_all.13 = bf16[4,128,2048]{2,1,0:T(8,128)(2,1)S(1)} all-to-all(bf16[4,128,2048]{2,1,0:T(8,128)(2,1)S(1)} %bitcast.16), channel_id=1, replica_groups=mesh['groups'=2,'fsdp'=4,'dp'=2,'pair'=2] {'fsdp'}, dimensions={0} | all-to-all | bytes 4194304 | tf_op jit(solution)/shard_map/all_to_all | solution.py:43
  91.1 0.5 convert_bitcast_fusion
  91.6 0.5 copy.10
  92.1 1.9 copy-done.1
  94.0 1.2 fusion
  95.2 2.2 fusion.10
  97.4 0.0 all-gather.2.cloned.1.call-start
  97.5 0.7 all-gather.2.cloned.1.call-update
  98.2 42.3 %reduce-scatter.2.cloned.1.call-done = f32[2048,64]{0,1:T(8,128)} async-done(((f32[8192,64]{0,1:T(8,128)}), f32[2048,64]{0,1:T(8,128)}) %reduce-scatter.2.cloned.1.call-update) | async-done | bytes 524304 | tf_op jit(solution)/shard_map/reduce_scatter | solution.py:58
  140.6 28.9 %all-gather.2.cloned.1.call-done = bf16[8192,64]{0,1:T(8,128)(2,1)} async-done(((bf16[2048,64]{0,1:T(8,128)(2,1)}), bf16[8192,64]{0,1:T(8,128)(2,1)}) %all-gather.2.cloned.1.call-update) | async-done | bytes 1048592 | tf_op jit(solution)/shard_map/all_gather | solution.py:49
  169.5 3.5 %convolution_multiply_fusion = f32[64,768]{1,0:T(8,128)} fusion(bf16[128,768]{1,0:T(8,128)(2,1)S(1)} %copy-done.4, bf16[8192,64]{0,1:T(8,128)(2,1)} %all-gather.2.cloned.1.call-done, bf16[128,8192]{1,0:T(8,128)(2,1)} %param.6, f32[8192]{0:T(1024)S(1)} %copy-done.5, f32[128]{0:T(128)S(1)} %get-tuple-element.5), kind=kOutput, calls=%fused_computation.13 | convolution fusion | flops 151052288 | bytes 3572224 | tf_op jit(solution)/shard_map/dot_general | solution.py:20
  173.1 5.3 %fusion.3 = bf16[128,8192]{1,0:T(8,128)(2,1)} fusion(bf16[128,8192]{1,0:T(8,128)(2,1)} %param.6, f32[128,8192]{1,0:T(8,128)} %bitcast.15, f32[128]{0:T(128)S(1)} %get-tuple-element.4, f32[128]{0:T(128)S(1)} %get-tuple-element.6, f32[8192]{0:T(1024)S(1)} %copy-done.5, f32[128]{0:T(128)S(1)} %get-tuple-element.5), kind=kLoop, calls=%fused_computation.7 | loop fusion | flops 7340032 | bytes 8422912 | tf_op jit(solution)/shard_map/convert_element_type | solution.py:66
  178.4 26.3 %all-reduce.3.cloned.1.call-done = f32[2048,64]{0,1:T(8,128)} async-done(((f32[2048,64]{0,1:T(8,128)}), f32[2048,64]{0,1:T(8,128)}) %all-reduce.3.cloned.1.call-update) | async-done | bytes 524304 | tf_op jit(solution)/shard_map/psum | solution.py:62
  204.7 1.8 multiply_reduce_fusion
  206.5 92.0 %all-reduce.5.cloned.1.call-done = f32[64,768]{1,0:T(8,128)} async-done(((f32[64,768]{1,0:T(8,128)}), f32[64,768]{1,0:T(8,128)}) %all-reduce.5.cloned.1.call-update) | async-done | bytes 196624 | tf_op jit(solution)/shard_map/psum | solution.py:63
  298.5 1.6 multiply_reduce_fusion.1
  300.1 11.2 %psum.22 = f32[]{:T(128)} all-reduce(f32[]{:T(128)} %multiply_reduce_fusion), channel_id=1, replica_groups=mesh['groups'=2,'fsdp'=4,'dp'=2,'pair'=2] {'fsdp'}, use_global_device_ids=true, to_apply=%region_5.0 | all-reduce | flops 1 | bytes 8 | tf_op jit(solution)/shard_map/psum | solution.py:64
  312.7 1.9 broadcast_multiply_fusion
  314.6 1.6 broadcast_multiply_fusion.1
  (18 shorter events, 0.2 us)
Async XLA Ops:
  7.2 34.9 %copy-start = (bf16[2048,768]{1,0:T(8,128)(2,1)S(1)}, bf16[2048,768]{1,0:T(8,128)(2,1)}, u32[]{:S(2)}) copy-start(bf16[2048,768]{1,0:T(8,128)(2,1)} %param.8) | copy-start | bytes 9437188
  7.2 133.4 %reduce-scatter.2.cloned.1.call-start = ((), (), s32[]{:S(2)}) async-start(), calls=%async_computation.2 | async-start | bytes 2621440 | tf_op jit(solution)/shard_map/reduce_scatter | solution.py:58
  42.1 1.8 copy-start.3
  91.6 2.5 copy-start.2
  91.6 2.4 copy-start.5
  92.1 1.9 copy-start.1
  95.2 74.3 %copy-start.4 = (bf16[128,768]{1,0:T(8,128)(2,1)S(1)}, bf16[128,768]{1,0:T(8,128)(2,1)}, u32[]{:S(2)}) copy-start(bf16[128,768]{1,0:T(8,128)(2,1)} %param.11) | copy-start | bytes 589828
  97.4 72.1 %all-gather.2.cloned.1.call-start = ((), (), s32[]{:S(2)}) async-start(), calls=%async_computation.4 | async-start | bytes 1310720 | tf_op jit(solution)/shard_map/all_gather | solution.py:49
  98.2 106.5 %all-reduce.3.cloned.1.call-start = ((), (), s32[]{:S(2)}) async-start(), calls=%async_computation.3 | async-start | bytes 1048576 | tf_op jit(solution)/shard_map/psum | solution.py:62
  140.6 157.9 %all-reduce.5.cloned.1.call-start = ((), (), s32[]{:S(2)}) async-start(), calls=%async_computation.5 | async-start | bytes 393216 | tf_op jit(solution)/shard_map/psum | solution.py:63
Sparse Core Ops, SparseCore 0:
  97.6 42.9 reduce-scatter.1
  142.2 27.2 all-gather.1
  172.0 32.6 all-reduce.2
  208.9 89.5 all-reduce.4
where the time goes:
time: 323 us
  waiting for transfers between devices  190 us (59%)
  blocking collectives  91.3 us (28%)
  between operations  15.2 us (5%)
  other arithmetic  13.9 us (4%)
  matrix products  9.43 us (3%)
    psum x1, waiting for transfers between devices, local(): up_full = lax.psum(up_portion, ('fsdp', 'dp', 'pair'))  92 us
    all_to_all x1, blocking collectives, local(): lax.all_to_all(columns.astype(jnp.bfloat16), 'fsdp', split_axis=0, concat...  46.4 us
    reduce_scatter x1, waiting for transfers between devices, local(): lax.psum_scatter(contract_leading(window, upward_product), 'fsdp', scatte...  42.3 us
    all_gather x1, waiting for transfers between devices, local(): lax.all_gather(adapter_down_map, 'fsdp', axis=0, tiled=True)  28.9 us
    psum x1, waiting for transfers between devices, local(): down_shard = lax.psum(down_shard, ('dp', 'pair'))  26.3 us
    all_gather x1, blocking collectives, local(): lax.all_gather(values_gradient, 'fsdp', axis=0, tiled=True)  21.6 us
    all_gather x1, blocking collectives, local(): lax.all_gather(upward_product, 'fsdp', axis=0, tiled=True)  12 us
    psum x1, blocking collectives, local(): lax.psum(jnp.sum(down_shard * down_shard), 'fsdp')  11.2 us
  transfers between devices with their start and end apart: 4, of which 4 were waited for; matrix products, arithmetic and copies ran while one was open for 3% of the time, Pallas kernels for 0%

commit v1 on v0

--- a/solution.py
+++ b/solution.py
@@ -60,7 +60,7 @@
     )
     up_portion = adapter_scale * contract_leading(latent_code, values_gradient)
     down_shard = lax.psum(down_shard, ("dp", "pair"))
-    up_full = lax.psum(up_portion, ("fsdp", "dp", "pair"))
+    up_full = jnp.sum(lax.all_gather(up_portion, ("fsdp", "dp", "pair")), axis=0)
     total = lax.psum(jnp.sum(down_shard * down_shard), "fsdp") + jnp.sum(up_full * up_full)
     factor = jnp.minimum(1.0, 0.5 * math.sqrt(MODEL_WIDTH * ADAPTER_RANK) / jnp.sqrt(total))
     return (grad_stream.astype(jnp.bfloat16), factor * down_shard, factor * up_full)

time: 323 us -> 266 us (0.82)
  waiting for transfers between devices: 190 us -> 132 us
    psum x1 -> x0, waiting for transfers between devices: 92 us -> none  [local(): up_full = lax.psum(up_portion, ('fsdp', 'dp', 'pair'))]
    all_gather x0 -> x1, waiting for transfers between devices: none -> 28.6 us  [local(): lax.all_gather(up_portion, ('fsdp', 'dp', 'pair'))]
    psum x1, waiting for transfers between devices: 26.3 us -> 31.6 us  [local(): down_shard = lax.psum(down_shard, ('dp', 'pair'))]
  transfers between devices with their start and end apart: 4 -> 4, of which waited for: 4 -> 4; matrix products, arithmetic and copies ran while one was open for 3% -> 4% of each run, Pallas kernels for 0% -> 0%
where the time goes in v1:
time: 266 us
  waiting for transfers between devices  132 us (50%)
  blocking collectives  92.4 us (35%)
  between operations  15.2 us (6%)
  other arithmetic  14.1 us (5%)
  matrix products  9.44 us (4%)
    all_to_all x1, blocking collectives, local(): lax.all_to_all(columns.astype(jnp.bfloat16), 'fsdp', split_axis=0, concat...  46.4 us
    reduce_scatter x1, waiting for transfers between devices, local(): lax.psum_scatter(contract_leading(window, upward_product), 'fsdp', scatte...  42.3 us
    psum x1, waiting for transfers between devices, local(): down_shard = lax.psum(down_shard, ('dp', 'pair'))  31.6 us
    all_gather x1, waiting for transfers between devices, local(): lax.all_gather(adapter_down_map, 'fsdp', axis=0, tiled=True)  28.9 us
    all_gather x1, waiting for transfers between devices, local(): lax.all_gather(up_portion, ('fsdp', 'dp', 'pair'))  28.6 us
    all_gather x1, blocking collectives, local(): lax.all_gather(values_gradient, 'fsdp', axis=0, tiled=True)  21.6 us
    psum x1, blocking collectives, local(): lax.psum(jnp.sum(down_shard * down_shard), 'fsdp')  12.4 us
    all_gather x1, blocking collectives, local(): lax.all_gather(upward_product, 'fsdp', axis=0, tiled=True)  12 us
  transfers between devices with their start and end apart: 4, of which 4 were waited for; matrix products, arithmetic and copies ran while one was open for 4% of the time, Pallas kernels for 0%

profile of v1, /device:TPU:0, one launch (start us, length us, event | category | flops | bytes accessed | tf_op | source)
XLA Modules:
  0.0 266.0 jit_solution(15390486985316888922)
XLA Ops:
  7.2 21.6 %all_gather.15 = bf16[512,768]{1,0:T(8,128)(2,1)S(1)} all-gather(bf16[128,768]{1,0:T(8,128)(2,1)} %param.11), channel_id=1, replica_groups=mesh['groups'=2,'fsdp'=4,'dp'=2,'pair'=2] {'fsdp'}, dimensions={0}, use_global_device_ids=true | all-gather | bytes 983040 | tf_op jit(solution)/shard_map/all_gather | solution.py:37
  28.9 1.2 fusion.7
  30.1 12.0 %all_gather.16 = bf16[512,64]{0,1:T(8,128)(2,1)S(1)} all-gather(bf16[128,64]{0,1:T(8,128)(2,1)S(1)} %fusion.7), channel_id=1, replica_groups=mesh['groups'=2,'fsdp'=4,'dp'=2,'pair'=2] {'fsdp'}, dimensions={0}, use_global_device_ids=true | all-gather | bytes 81920 | tf_op jit(solution)/shard_map/all_gather | solution.py:38
  42.1 1.8 fusion.13
  43.9 0.7 add_convert_fusion
  44.6 46.4 %all_to_all.13 = bf16[4,128,2048]{2,1,0:T(8,128)(2,1)S(1)} all-to-all(bf16[4,128,2048]{2,1,0:T(8,128)(2,1)S(1)} %bitcast.17), channel_id=1, replica_groups=mesh['groups'=2,'fsdp'=4,'dp'=2,'pair'=2] {'fsdp'}, dimensions={0} | all-to-all | bytes 4194304 | tf_op jit(solution)/shard_map/all_to_all | solution.py:43
  91.1 0.5 convert_bitcast_fusion
  91.6 0.5 copy.10
  92.1 1.9 copy-done.1
  94.0 1.2 fusion
  95.3 2.2 fusion.10
  97.5 0.7 all-gather.4.cloned.1.call-update
  98.2 42.3 %reduce-scatter.2.cloned.1.call-done = f32[2048,64]{0,1:T(8,128)} async-done(((f32[8192,64]{0,1:T(8,128)}), f32[2048,64]{0,1:T(8,128)}) %reduce-scatter.2.cloned.1.call-update) | async-done | bytes 524304 | tf_op jit(solution)/shard_map/reduce_scatter | solution.py:58
  140.6 28.9 %all-gather.4.cloned.1.call-done = bf16[8192,64]{0,1:T(8,128)(2,1)} async-done(((bf16[2048,64]{0,1:T(8,128)(2,1)}), bf16[8192,64]{0,1:T(8,128)(2,1)}) %all-gather.4.cloned.1.call-update) | async-done | bytes 1048592 | tf_op jit(solution)/shard_map/all_gather | solution.py:49
  169.5 3.5 %convolution_multiply_fusion = f32[64,768]{1,0:T(8,128)} fusion(bf16[128,768]{1,0:T(8,128)(2,1)S(1)} %copy-done.4, bf16[8192,64]{0,1:T(8,128)(2,1)} %all-gather.4.cloned.1.call-done, bf16[128,8192]{1,0:T(8,128)(2,1)} %param.6, f32[8192]{0:T(1024)S(1)} %copy-done.5, f32[128]{0:T(128)S(1)} %get-tuple-element.5), kind=kOutput, calls=%fused_computation.13 | convolution fusion | flops 151052288 | bytes 3572224 | tf_op jit(solution)/shard_map/dot_general | solution.py:20
  173.1 31.6 %all-reduce.2.cloned.1.call-done = f32[2048,64]{0,1:T(8,128)} async-done(((f32[2048,64]{0,1:T(8,128)}), f32[2048,64]{0,1:T(8,128)}) %all-reduce.2.cloned.1.call-update) | async-done | bytes 524304 | tf_op jit(solution)/shard_map/psum | solution.py:62
  204.7 1.8 multiply_reduce_fusion
  206.5 5.3 %fusion.3 = bf16[128,8192]{1,0:T(8,128)(2,1)} fusion(bf16[128,8192]{1,0:T(8,128)(2,1)} %param.6, f32[128,8192]{1,0:T(8,128)} %bitcast.16, f32[128]{0:T(128)S(1)} %get-tuple-element.4, f32[128]{0:T(128)S(1)} %get-tuple-element.6, f32[8192]{0:T(1024)S(1)} %copy-done.5, f32[128]{0:T(128)S(1)} %get-tuple-element.5), kind=kLoop, calls=%fused_computation.7 | loop fusion | flops 7340032 | bytes 8422912 | tf_op jit(solution)/shard_map/convert_element_type | solution.py:66
  211.8 12.4 %psum.15 = f32[]{:T(128)} all-reduce(f32[]{:T(128)} %multiply_reduce_fusion), channel_id=1, replica_groups=mesh['groups'=2,'fsdp'=4,'dp'=2,'pair'=2] {'fsdp'}, use_global_device_ids=true, to_apply=%region_5.0 | all-reduce | flops 1 | bytes 8 | tf_op jit(solution)/shard_map/psum | solution.py:64
  224.2 28.6 %all-gather.6.cloned.1.call-done = f32[1024,768]{1,0:T(8,128)} async-done(((f32[64,768]{1,0:T(8,128)}), f32[1024,768]{1,0:T(8,128)}) %all-gather.6.cloned.1.call-update) | async-done | bytes 3145744 | tf_op jit(solution)/shard_map/all_gather | solution.py:63
  252.8 2.1 reduce_sum.48
  254.9 0.6 multiply_reduce_fusion.1
  256.9 0.7 broadcast_multiply_fusion.1
  257.6 1.9 broadcast_multiply_fusion
  (19 shorter events, 0.2 us)
Async XLA Ops:
  7.2 34.9 %copy-start = (bf16[2048,768]{1,0:T(8,128)(2,1)S(1)}, bf16[2048,768]{1,0:T(8,128)(2,1)}, u32[]{:S(2)}) copy-start(bf16[2048,768]{1,0:T(8,128)(2,1)} %param.8) | copy-start | bytes 9437188
  7.2 133.4 %reduce-scatter.2.cloned.1.call-start = ((), (), s32[]{:S(2)}) async-start(), calls=%async_computation.2 | async-start | bytes 2621440 | tf_op jit(solution)/shard_map/reduce_scatter | solution.py:58
  42.1 1.8 copy-start.3
  91.6 2.5 copy-start.2
  91.6 2.4 copy-start.5
  92.1 1.9 copy-start.1
  95.2 74.3 %copy-start.4 = (bf16[128,768]{1,0:T(8,128)(2,1)S(1)}, bf16[128,768]{1,0:T(8,128)(2,1)}, u32[]{:S(2)}) copy-start(bf16[128,768]{1,0:T(8,128)(2,1)} %param.11) | copy-start | bytes 589828
  97.4 72.1 %all-gather.4.cloned.1.call-start = ((), (), s32[]{:S(2)}) async-start(), calls=%async_computation.4 | async-start | bytes 1310720 | tf_op jit(solution)/shard_map/all_gather | solution.py:49
  98.2 106.5 %all-reduce.2.cloned.1.call-start = ((), (), s32[]{:S(2)}) async-start(), calls=%async_computation.3 | async-start | bytes 1048576 | tf_op jit(solution)/shard_map/psum | solution.py:62
  140.6 112.2 %all-gather.6.cloned.1.call-start = ((), (), s32[]{:S(2)}) async-start(), calls=%async_computation.5 | async-start | bytes 3342336 | tf_op jit(solution)/shard_map/all_gather | solution.py:63
Sparse Core Ops, SparseCore 0:
  97.6 42.9 reduce-scatter.1
  142.2 27.2 all-gather.3
  172.0 32.6 all-reduce.1
  207.7 45.1 all-gather.5
